TPU v7x, 32 devices: a whole 2x2x4 slice. The times are simulated.
32 devices in a mesh: face: 4 (over x, core), tile: 2 (over y), dp: 4 (over z).
Axes of the slice: x: 2, y: 2, z: 4, core: 2. Of those that a mesh axis runs over, the one named last changes fastest.
Arguments:
- inputs: bfloat16 [4, 8, 32, 32, 128], P('dp', ('face', 'tile')), may hold values from -6 to 6
- weight: bfloat16 [9, 128, 128], replicated, may hold values from -0.1875 to 0.1875
- bias: float32 [128], replicated, may hold values from -3 to 3
- seam: int32 [6, 4, 3], replicated, may hold values from 0 to 5, as said below
- station_grad: bfloat16 [4, 1024, 128], P('dp', ('face', 'tile')), may hold values from -6 to 6
- station_tile: int32 [1024, 1], P(('face', 'tile')), may hold values from 0 to 5; in each aligned block of 128 rows (0 to 127, 128 to 255, ...) at most 42 rows name the same one
- station_cell: int32 [1024], P(('face', 'tile')), may hold values from 0 to 1023
Outputs:
- forward: bfloat16 [4, 8, 32, 32, 128], P('dp', ('face', 'tile'))
- input_grad: bfloat16 [4, 8, 32, 32, 128], P('dp', ('face', 'tile'))
- weight_grad: float32 [9, 128, 128], replicated
- bias_grad: float32 [128], replicated
Inputs may be any that keep to these rules, and one draw needn't show every extreme that they name: seam glues the 6 panels as the faces of a cube: seam[q, e] = (q2, e2, f) glues side e of panel q to side e2 of panel q2, reversed if f = 1; then seam[q2, e2] = (q, e, f); no panel is glued to itself. Entries 0 and 1 name panels and sides, entry 2 is 0 or 1. `station_tile`: among the 128 stations of one device (aligned blocks of the list), at most 42 lie in any one tile.
All inputs are finite; a program needn't handle non-finite values.
Results may differ from a plain program's by a relative error of at most 0.006.
Values may be sent and summed in bfloat16 or wider, within the bound.
A program may use at most 64 MiB of HBM per device.

v0:
```python
import math

import jax
import jax.numpy as jnp
import numpy as np
from jax import lax
from jax.sharding import PartitionSpec as P

ST_DEV = 128


def seam_pad(field, seam):
    extent, channels = (field.shape[0], field.shape[2])
    tiles_here = lax.axis_size("tile")
    tile_grid = math.isqrt(tiles_here // 2)
    tile_count = tile_grid * tile_grid
    line_length = tile_grid * extent
    last_panel = seam.shape[0] - 1
    strips = jnp.stack([field[0], field[-1], field[:, 0], field[:, -1]], axis=0)
    all_strips = lax.all_gather(strips[None], "tile", axis=0, tiled=True)
    lines = []
    for side_id in range(4):
        tile_ids = np.zeros((2, tile_grid), np.int32)
        for panel_half in range(2):
            for offset in range(tile_grid):
                if side_id == 0:
                    local = offset
                elif side_id == 1:
                    local = (tile_grid - 1) * tile_grid + offset
                elif side_id == 2:
                    local = offset * tile_grid
                else:
                    local = offset * tile_grid + tile_grid - 1
                tile_ids[panel_half, offset] = panel_half * tile_count + local
        lines.append(all_strips[tile_ids, side_id].reshape(2, line_length, channels))
    perimeter = jnp.stack(lines, axis=1)
    position = lax.axis_index("tile")
    panel_half = position // tile_count
    tile_row = position % tile_count // tile_grid
    tile_col = position % tile_grid
    face_id = lax.axis_index("face")
    panel = jnp.minimum(face_id * 2 + panel_half, last_panel)
    steps = [-tile_grid, tile_grid, -1, 1]
    facing = [1, 0, 3, 2]
    border = [tile_row == 0, tile_row == tile_grid - 1, tile_col == 0, tile_col == tile_grid - 1]
    along = [tile_col, tile_col, tile_row, tile_row]
    segments = []
    side_lines = lax.all_gather(perimeter, "face", axis=0, tiled=True)
    for side_id in range(4):
        seam_row = seam[panel, side_id]
        side_line = side_lines[seam_row[0], seam_row[1]]
        side_line = jnp.where(seam_row[2] == 1, side_line[::-1], side_line)
        segments.append(lax.dynamic_slice_in_dim(side_line, along[side_id] * extent, extent, 0))
    rims = []
    for side_id in range(4):
        beside = jnp.clip(position + steps[side_id], 0, tiles_here - 1)
        inside = lax.dynamic_index_in_dim(all_strips, beside, 0, keepdims=False)[facing[side_id]]
        rims.append(jnp.where(border[side_id], segments[side_id], inside))
    zero_cell = jnp.zeros((1, channels), field.dtype)
    middle = jnp.concatenate([rims[2][:, None], field, rims[3][:, None]], axis=1)
    top_row = jnp.concatenate([zero_cell, rims[0], zero_cell], axis=0)[None]
    bottom_row = jnp.concatenate([zero_cell, rims[1], zero_cell], axis=0)[None]
    return jnp.concatenate([top_row, middle, bottom_row], axis=0)


def convolve(padded, kernel):
    return lax.conv_general_dilated(
        padded[None],
        kernel,
        (1, 1),
        "VALID",
        dimension_numbers=("NHWC", "HWIO", "NHWC"),
        preferred_element_type=jnp.float32,
    )[0]


def body(inputs, weight, bias, seam, station_grad, station_tile, station_cell):
    field = inputs[0, 0]
    extent, channels = (field.shape[0], field.shape[2])
    tile_grid = math.isqrt(lax.axis_size("tile") // 2)
    tiles_real = seam.shape[0] * tile_grid * tile_grid
    active = lax.axis_index(("face", "tile")) < tiles_real
    kernel = weight.reshape(3, 3, channels, channels)
    flipped = jnp.transpose(kernel[::-1, ::-1], (0, 1, 3, 2))
    padded = seam_pad(field, seam)
    preact = convolve(padded, kernel) + bias
    gating = jax.nn.sigmoid(preact)
    output = (preact * gating).astype(jnp.bfloat16)
    output = jnp.where(active, output, jnp.zeros_like(output))
    station_vals = station_grad[0]
    owners = station_tile[:, 0]
    cell_total = extent * extent
    empty = jnp.zeros((cell_total, channels), jnp.float32)
    my_tile = lax.axis_index(("face", "tile"))
    values = lax.all_gather(station_vals, ("face", "tile"), axis=0, tiled=True)
    tiles_of = lax.all_gather(owners, ("face", "tile"), axis=0, tiled=True)
    cells_of = lax.all_gather(station_cell, ("face", "tile"), axis=0, tiled=True)
    target = jnp.where(tiles_of == my_tile, cells_of, cell_total)
    grad_out = empty.at[target].add(values.astype(jnp.float32), mode="drop")
    grad_out = grad_out.reshape(extent, extent, channels)
    grad_pre = (grad_out * gating * (1.0 + preact * (1.0 - gating))).astype(jnp.bfloat16)
    grad_in = convolve(seam_pad(grad_pre, seam), flipped).astype(jnp.bfloat16)
    grad_in = jnp.where(active, grad_in, jnp.zeros_like(grad_in))
    taps = []
    for tap_row in range(3):
        for tap_col in range(3):
            window = padded[tap_row : tap_row + extent, tap_col : tap_col + extent]
            taps.append(
                jnp.einsum("ijc,ijo->co", window, grad_pre, preferred_element_type=jnp.float32)
            )
    grad_weight = jnp.stack(taps, axis=0)
    grad_bias = jnp.sum(grad_pre.astype(jnp.float32), axis=(0, 1))
    grad_weight = jnp.where(active, grad_weight, jnp.zeros_like(grad_weight))
    grad_bias = jnp.where(active, grad_bias, jnp.zeros_like(grad_bias))
    grad_weight, grad_bias = lax.psum((grad_weight, grad_bias), ("face", "tile", "dp"))
    factor = 1.0 / math.sqrt(
        lax.axis_size("dp") * ST_DEV * lax.axis_size("face") * lax.axis_size("tile")
    )
    return (output[None, None], grad_in[None, None], grad_weight * factor, grad_bias * factor)


def solution(mesh):
    return jax.shard_map(
        body,
        mesh=mesh,
        in_specs=(
            P("dp", ("face", "tile"), None, None, None),
            P(),
            P(),
            P(),
            P("dp", ("face", "tile"), None),
            P(("face", "tile"), None),
            P(("face", "tile")),
        ),
        out_specs=(
            P("dp", ("face", "tile"), None, None, None),
            P("dp", ("face", "tile"), None, None, None),
            P(),
            P(),
        ),
        check_vma=False,
    )
```

profile of v0, /device:TPU:0, one launch (start us, length us, event | category | flops | bytes accessed | tf_op | source)
XLA Modules:
  0.0 233.6 jit_solution(12656369021577688890)
XLA Ops:
  7.2 0.7 copy-done.6
  8.0 0.7 constant_dynamic-slice_fusion.1
  21.2 0.7 slice_bitcast_fusion.4
  21.9 0.9 fusion.64
  22.9 5.5 %all-gather = bf16[8,32,128]{2,1,0:T(8,128)(2,1)S(1)} all-gather(bf16[4,32,128]{2,1,0:T(8,128)(2,1)S(1)} %pad_maximum_fusion.7), channel_id=2, replica_groups=mesh['face'=4,'tile'=2,'dp'=4] {'tile'}, dimensions={0}, use_global_device_ids=true | all-gather | bytes 98304 | tf_op jit(solution)/shard_map/all_gather | solution.py:20
  28.4 0.7 copy-done.5
  29.0 0.6 gather_fusion.3
  29.7 0.6 gather_fusion.2
  30.3 0.6 gather_fusion.1
  30.9 0.6 gather_fusion
  31.5 6.4 %all_gather.22 = bf16[8,4,32,128]{3,2,1,0:T(8,128)(2,1)S(1)} all-gather(bf16[2,4,32,128]{3,2,1,0:T(8,128)(2,1)S(1)} %pad_maximum_fusion.5), channel_id=1, replica_groups=mesh['face'=4,'tile'=2,'dp'=4] {'face'}, dimensions={0}, use_global_device_ids=true | all-gather | bytes 327680 | tf_op jit(solution)/shard_map/all_gather | solution.py:48
  44.0 11.9 %all-gather.1 = s32[1024,1]{0,1:T(1,128)S(1)} all-gather(s32[128,1]{0,1:T(1,128)S(1)} %copy-done.8), channel_id=3, replica_groups=mesh['face'=4,'tile'=2,'dp'=4] {'face','tile'}, dimensions={0}, use_global_device_ids=true | all-gather | bytes 4608 | tf_op jit(solution)/shard_map/all_gather | solution.py:96
  55.9 0.6 copy-done.9
  56.5 10.9 %all-gather.4 = s32[8,1,128]{2,1,0:T(1,128)S(1)} all-gather(s32[1,1,128]{2,1,0:T(1,128)S(1)} %bitcast.194), channel_id=1, replica_groups=mesh['face'=4,'tile'=2,'dp'=4] {'face','tile'}, dimensions={0}, use_global_device_ids=true | all-gather | bytes 4608 | tf_op jit(solution)/shard_map/all_gather | solution.py:97
  67.5 16.2 %all-gather.2 = bf16[1,1024,128]{2,1,0:T(8,128)(2,1)S(1)} all-gather(bf16[1,128,128]{2,1,0:T(8,128)(2,1)S(1)} %copy-done.2), channel_id=4, replica_groups=mesh['face'=4,'tile'=2,'dp'=4] {'face','tile'}, dimensions={1}, use_global_device_ids=true | all-gather | bytes 294912 | tf_op jit(solution)/shard_map/all_gather | solution.py:95
  83.9 0.7 copy-done.10
  84.6 0.9 convolution_select_fusion.1
  86.0 6.2 %scatter_custom_fusion = f32[1024,128]{1,0:T(8,128)S(1)} fusion(s32[1024]{0:T(1024)S(1)} %compare_select_fusion, bf16[1,1024,128]{2,1,0:T(8,128)(2,1)S(1)} %all-gather.2, f32[]{:T(128)} %constant.115.clone.1), kind=kCustom, calls=%fused_computation.34 | custom fusion | flops 262144 | bytes 786436 | tf_op jit(solution)/shard_map/scatter-add | solution.py:99
  92.3 0.6 copy-done.7
  96.1 0.9 broadcast_select_fusion
  97.1 4.6 %all-gather.3 = bf16[8,32,128]{2,1,0:T(8,128)(2,1)S(1)} all-gather(bf16[4,32,128]{2,1,0:T(8,128)(2,1)S(1)} %pad_maximum_fusion.8), channel_id=5, replica_groups=mesh['face'=4,'tile'=2,'dp'=4] {'tile'}, dimensions={0}, use_global_device_ids=true | all-gather | bytes 98304 | tf_op jit(solution)/shard_map/all_gather | solution.py:20
  101.7 0.6 gather_fusion.4
  102.3 0.6 gather_fusion.7
  102.8 0.6 gather_fusion.6
  103.4 0.6 gather_fusion.5
  104.2 6.0 %all_gather.27 = bf16[8,4,32,128]{3,2,1,0:T(8,128)(2,1)S(1)} all-gather(bf16[2,4,32,128]{3,2,1,0:T(8,128)(2,1)S(1)} %pad_maximum_fusion.6), channel_id=1, replica_groups=mesh['face'=4,'tile'=2,'dp'=4] {'face'}, dimensions={0}, use_global_device_ids=true | all-gather | bytes 327680 | tf_op jit(solution)/shard_map/all_gather | solution.py:48
  110.6 0.9 fusion.1
  111.7 0.8 copy.112
  112.5 0.8 copy.113
  113.3 39.7 %psum.15 = f32[128]{0:T(128)S(1)} all-reduce(f32[128]{0:T(128)S(1)} %broadcast_select_fusion.5), channel_id=1, replica_groups=mesh['face'=4,'tile'=2,'dp'=4] {'face','tile','dp'}, use_global_device_ids=true, to_apply=%region_3.4 | all-reduce | flops 128 | bytes 1024 | tf_op jit(solution)/shard_map/psum | solution.py:115
  153.5 71.4 %all-reduce.10.cloned.1.call-done = f32[9,128,128]{2,1,0:T(8,128)} async-done(((f32[9,128,128]{2,1,0:T(8,128)}), f32[9,128,128]{2,1,0:T(8,128)}) %all-reduce.10.cloned.1.call-update) | async-done | bytes 589840 | tf_op jit(solution)/shard_map/psum | solution.py:115
  224.9 1.9 broadcast_multiply_fusion
  (85 shorter events, 6.4 us)
Async XLA Ops:
  7.2 76.7 %copy-start = (bf16[9,128,128]{2,1,0:T(8,128)(2,1)S(1)}, bf16[9,128,128]{2,1,0:T(8,128)(2,1)}, u32[]{:S(2)}) copy-start(bf16[9,128,128]{2,1,0:T(8,128)(2,1)} %param.24) | copy-start | bytes 884740
  7.2 217.7 %all-reduce.10.cloned.1.call-start = ((), (), s32[]{:S(2)}) async-start(), calls=%async_computation | async-start | bytes 1179648 | tf_op jit(solution)/shard_map/psum | solution.py:115
  7.2 0.7 copy-start.6
  28.4 0.7 copy-start.5
  29.0 0.7 copy-start.4
  29.7 0.7 copy-start.3
  31.5 11.7 %copy-start.1 = (bf16[1,1,32,32,128]{4,3,2,1,0:T(8,128)(2,1)S(1)}, bf16[1,1,32,32,128]{4,3,2,1,0:T(8,128)(2,1)}, u32[]{:S(2)}) copy-start(bf16[1,1,32,32,128]{4,3,2,1,0:T(8,128)(2,1)} %param.23) | copy-start | bytes 786436
  43.3 0.7 copy-start.8
  43.3 24.1 %copy-start.2 = (bf16[1,128,128]{2,1,0:T(8,128)(2,1)S(1)}, bf16[1,128,128]{2,1,0:T(8,128)(2,1)}, u32[]{:S(2)}) copy-start(bf16[1,128,128]{2,1,0:T(8,128)(2,1)} %param.27) | copy-start | bytes 98308
  55.9 0.7 copy-start.9
  83.9 0.7 copy-start.10
  92.2 0.7 copy-start.7
Sparse Core Ops, SparseCore 0:
  97.1 127.6 all-reduce.9
where the time goes:
time: 234 us
  blocking collectives  101 us (43%)
  waiting for transfers between devices  71.4 us (31%)
  between operations  32 us (14%)
  local copies, waits for them, and re-layouts  13.6 us (6%)
  other arithmetic  11 us (5%)
  matrix products  4.41 us (2%)
    psum x1, waiting for transfers between devices, body(): lax.psum((grad_weight, grad_bias), ('face', 'tile', 'dp'))  71.4 us
    psum x1, blocking collectives, body(): lax.psum((grad_weight, grad_bias), ('face', 'tile', 'dp'))  39.7 us
    all_gather x1, blocking collectives, body(): values = lax.all_gather(station_vals, ('face', 'tile'), axis=0, tiled=True)  16.2 us
    all_gather x2, blocking collectives, seam_pad(): side_lines = lax.all_gather(perimeter, 'face', axis=0, tiled=True)  12.4 us
    all_gather x1, blocking collectives, body(): tiles_of = lax.all_gather(owners, ('face', 'tile'), axis=0, tiled=True)  11.9 us
    all_gather x1, blocking collectives, body(): lax.all_gather(station_cell, ('face', 'tile'), axis=0, tiled=True)  10.9 us
    all_gather x2, blocking collectives, seam_pad(): all_strips = lax.all_gather(strips[None], 'tile', axis=0, tiled=True)  10.1 us
    scatter-add x1, other arithmetic, body(): grad_out = empty.at[target].add(values.astype(jnp.float32), mode='drop')  6.19 us
  transfers between devices with their start and end apart: 1, of which 1 were waited for; matrix products, arithmetic and copies ran while one was open for 3% of the time, Pallas kernels for 0%

commit v1 on v0

v1 whole, which is shorter than its diff:
```python
import math

import jax
import jax.numpy as jnp
from jax import lax
from jax.sharding import PartitionSpec as P

GROUP = ("face", "tile")


def edge_strips(field):
    return jnp.stack([field[0], field[-1], field[:, 0], field[:, -1]], axis=0)


def rim_sources(seam):
    tiles_here = lax.axis_size("tile")
    grid = math.isqrt(tiles_here // 2)
    count = grid * grid
    slot = jnp.minimum(lax.axis_index(GROUP), seam.shape[0] * count - 1)
    panel, local = slot // count, slot % count
    row, col = local // grid, local % grid
    border = [row == 0, row == grid - 1, col == 0, col == grid - 1]
    steps, facing, along = [-grid, grid, -1, 1], [1, 0, 3, 2], [col, col, row, row]
    out = []
    for e in range(4):
        q, side, flag = seam[panel, e, 0], seam[panel, e, 1], seam[panel, e, 2]
        k = jnp.where(flag == 1, grid - 1 - along[e], along[e])
        far = jnp.where(
            side == 0, k, jnp.where(side == 1, (grid - 1) * grid + k,
                                    jnp.where(side == 2, k * grid, k * grid + grid - 1)))
        out.append((
            jnp.where(border[e], q * count + far, slot + steps[e]),
            jnp.where(border[e], side, facing[e]),
            border[e] & (flag == 1),
        ))
    return out


def pad(field, gathered, sources):
    rims = []
    for slot, side, flip in sources:
        strip = lax.dynamic_slice(
            gathered, (slot, side, 0, 0), (1, 1) + gathered.shape[2:])[0, 0]
        rims.append(jnp.where(flip, strip[::-1], strip))
    zero = jnp.zeros((1, field.shape[2]), field.dtype)
    middle = jnp.concatenate([rims[2][:, None], field, rims[3][:, None]], axis=1)
    top = jnp.concatenate([zero, rims[0], zero], axis=0)[None]
    bottom = jnp.concatenate([zero, rims[1], zero], axis=0)[None]
    return jnp.concatenate([top, middle, bottom], axis=0)


def patches(padded):
    s = padded.shape[0] - 2
    return jnp.concatenate(
        [padded[a : a + s, b : b + s] for a in range(3) for b in range(3)], axis=-1
    ).reshape(s * s, -1)


def body(inputs, weight, bias, seam, station_grad, station_tile, station_cell):
    field = inputs[0, 0]
    s, c = field.shape[0], field.shape[2]
    grid = math.isqrt(lax.axis_size("tile") // 2)
    slots = lax.axis_size(GROUP)
    stations = station_cell.shape[0]
    me = lax.axis_index(GROUP)
    active = me < seam.shape[0] * grid * grid
    sources = rim_sources(seam)

    sent = jnp.concatenate([edge_strips(field).reshape(4 * s, c), station_grad[0]], axis=0)
    got = lax.all_gather(sent, GROUP, axis=0)
    key = station_tile[:, 0] * (s * s) + station_cell
    keys = lax.all_gather(key, GROUP, axis=0, tiled=True)
    lines = got[:, : 4 * s].reshape(slots, 4, s, c)
    values = got[:, 4 * s :].reshape(slots * stations, c)

    cols = patches(pad(field, lines, sources))
    preact = jnp.dot(cols, weight.reshape(9 * c, c), preferred_element_type=jnp.float32) + bias
    gate = jax.nn.sigmoid(preact)
    output = jnp.where(active, preact * gate, 0.0).astype(jnp.bfloat16).reshape(field.shape)

    cells = me * (s * s) + lax.broadcasted_iota(jnp.int32, (s * s, 1), 0)
    hits = (cells == keys[None, :]).astype(jnp.bfloat16)
    grad_out = jnp.dot(hits, values, preferred_element_type=jnp.float32)
    grad_pre = (grad_out * gate * (1.0 + preact * (1.0 - gate))).astype(jnp.bfloat16)

    grad_field = grad_pre.reshape(field.shape)
    edges = lax.all_gather(edge_strips(grad_field), GROUP, axis=0)
    flipped = jnp.transpose(weight[::-1], (0, 2, 1)).reshape(9 * c, c)
    grad_in = jnp.dot(
        patches(pad(grad_field, edges, sources)), flipped, preferred_element_type=jnp.float32)
    grad_in = jnp.where(active, grad_in, 0.0).astype(jnp.bfloat16).reshape(field.shape)

    grad_w = lax.dot_general(
        cols, grad_pre, (((0,), (0,)), ((), ())), preferred_element_type=jnp.float32)
    grad_b = jnp.sum(grad_pre.astype(jnp.float32), axis=0, keepdims=True)
    terms = jnp.concatenate([grad_w, jnp.broadcast_to(grad_b, (8, c))], axis=0)
    terms = jnp.where(active, terms, 0.0)
    total = lax.psum(terms, ("face", "tile", "dp"))
    total = total / math.sqrt(lax.axis_size("dp") * slots * stations)
    return (output[None, None], grad_in[None, None],
            total[: 9 * c].reshape(9, c, c), total[9 * c])


def solution(mesh):
    return jax.shard_map(
        body,
        mesh=mesh,
        in_specs=(
            P("dp", GROUP, None, None, None),
            P(),
            P(),
            P(),
            P("dp", GROUP, None),
            P(GROUP, None),
            P(GROUP),
        ),
        out_specs=(
            P("dp", GROUP, None, None, None),
            P("dp", GROUP, None, None, None),
            P(),
            P(),
        ),
        check_vma=False,
    )
```

time: 234 us -> 207 us (0.88)
  blocking collectives: 101 us -> 45.8 us
  waiting for transfers between devices: 71.4 us -> 103 us
  other arithmetic: 11 us -> 3.7 us
    psum x1 -> x0, blocking collectives: 39.7 us -> none  [body(): lax.psum((grad_weight, grad_bias), ('face', 'tile', 'dp'))]
    psum x1, waiting for transfers between devices: 71.4 us -> 103 us  [body(): total = lax.psum(terms, ('face', 'tile', 'dp'))]
    all_gather x7 -> x3, blocking collectives: 61.5 us -> 45.8 us  [the longest x1 18.9 us: body(): got = lax.all_gather(sent, GROUP, axis=0)]
    scatter-add x1 -> x0, other arithmetic: 6.19 us -> none  [body(): grad_out = empty.at[target].add(values.astype(jnp.float32), mode='drop')]
    gather x8 -> x0, local copies, waits for them, and re-layouts: 4.49 us -> none  [seam_pad(): all_strips[tile_ids, side_id].reshape(2, line_length, channels)]
    dot_general x9 -> x4, matrix products: 2.53 us -> 6.39 us  [the longest x1 3.16 us: body(): jnp.dot(patches(pad(grad_field, edges, sources)), flipped, preferred_elem...]
    slice x4 -> x10, local copies, waits for them, and re-layouts: 2.35 us -> 5.42 us  [the longest x4 2.16 us: patches(): padded[a:a + s, b:b + s]]
    mul x2 -> x0, other arithmetic: 2.43 us -> none  [the longest x1 1.92 us: body(): grad_weight * factor]
  transfers between devices with their start and end apart: 1 -> 1, of which waited for: 1 -> 1; matrix products, arithmetic and copies ran while one was open for 3% -> 4% of each run, Pallas kernels for 0% -> 0%
where the time goes in v1:
time: 207 us; the launch traced here: 206 us
  waiting for transfers between devices  103 us (50%)
  blocking collectives  45.8 us (22%)
  between operations  32.2 us (16%)
  local copies, waits for them, and re-layouts  15.3 us (7%)
  matrix products  6.39 us (3%)
  other arithmetic  3.7 us (2%)
    psum x1, waiting for transfers between devices, body(): total = lax.psum(terms, ('face', 'tile', 'dp'))  103 us
    all_gather x1, blocking collectives, body(): got = lax.all_gather(sent, GROUP, axis=0)  18.9 us
    all_gather x1, blocking collectives, body(): edges = lax.all_gather(edge_strips(grad_field), GROUP, axis=0)  15.7 us
    all_gather x1, blocking collectives, body(): keys = lax.all_gather(key, GROUP, axis=0, tiled=True)  11.2 us
    unnamed x40, local copies, waits for them, and re-layouts  6.61 us
  transfers between devices with their start and end apart: 1, of which 1 were waited for; matrix products, arithmetic and copies ran while one was open for 4% of the time, Pallas kernels for 0%

profile of v1, /device:TPU:0, one launch (start us, length us, event | category | flops | bytes accessed | tf_op | source)
XLA Modules:
  0.0 206.1 jit_solution(10399887155623754747)
XLA Ops:
  7.2 1.6 constant_dynamic-slice_fusion.7
  18.9 0.7 slice_bitcast_fusion.3
  19.6 0.9 fusion.25
  20.5 0.8 pad_maximum_fusion.6
  21.3 18.9 %all-gather = bf16[2048,128]{1,0:T(8,128)(2,1)S(1)} all-gather(bf16[256,128]{1,0:T(8,128)(2,1)S(1)} %pad_maximum_fusion.6), channel_id=2, replica_groups=mesh['face'=4,'tile'=2,'dp'=4] {'face','tile'}, dimensions={0}, use_global_device_ids=true | all-gather | bytes 589824 | tf_op jit(solution)/shard_map/all_gather | solution.py:70
  40.2 0.7 fusion.19
  48.8 0.2 pad_maximum_fusion.4
  49.1 0.2 pad_maximum_fusion
  49.3 1.0 fusion.23
  50.3 0.9 fusion.22
  51.3 11.2 %all-gather.2 = s32[8,1,128]{2,1,0:T(1,128)S(1)} all-gather(s32[1,1,128]{2,1,0:T(1,128)S(1)} %fusion.18), channel_id=1, replica_groups=mesh['face'=4,'tile'=2,'dp'=4] {'face','tile'}, dimensions={0}, use_global_device_ids=true | all-gather | bytes 4608 | tf_op jit(solution)/shard_map/all_gather | solution.py:72
  62.5 1.0 constant_dynamic-update-slice_fusion.7
  63.5 1.0 constant_dynamic-update-slice_fusion.6
  65.0 1.5 select_convert_fusion
  66.5 0.9 convert_reduce_fusion
  67.4 0.8 fusion.26
  68.2 0.9 maximum_select_fusion
  69.2 0.2 copy.57
  69.5 15.7 %all-gather.1 = bf16[32,32,128]{2,1,0:T(8,128)(2,1)S(1)} all-gather(bf16[4,32,128]{2,1,0:T(8,128)(2,1)S(1)} %pad_maximum_fusion.8), channel_id=3, replica_groups=mesh['face'=4,'tile'=2,'dp'=4] {'face','tile'}, dimensions={0}, use_global_device_ids=true | all-gather | bytes 294912 | tf_op jit(solution)/shard_map/all_gather | solution.py:87
  85.4 0.2 pad_maximum_fusion.2
  85.6 0.2 pad_maximum_fusion.1
  85.8 0.2 fusion.21
  86.3 1.4 copy-done.6
  88.0 0.7 constant_dynamic-update-slice_fusion.12
  88.7 0.7 constant_dynamic-update-slice_fusion.11
  89.4 0.7 constant_dynamic-update-slice_fusion.10
  90.2 0.8 constant_dynamic-update-slice_fusion.9
  90.9 3.2 %fusion.13 = bf16[1024,128]{1,0:T(8,128)(2,1)} fusion(bf16[1024,1152]{1,0:T(8,128)(2,1)} %constant_dynamic-update-slice_fusion.9, bf16[1152,128]{1,0:T(8,128)(2,1)S(1)} %bitcast.138, pred[]{:T(512)S(6)} %lt.26), kind=kOutput, calls=%fused_computation.9 | convolution fusion | flops 302252032 | bytes 2916353 | tf_op jit(solution)/shard_map/dot_general | solution.py:89
  94.1 102.7 %all-reduce.2.cloned.1.call-done = f32[1160,128]{1,0:T(8,128)} async-done(((f32[1160,128]{1,0:T(8,128)}), f32[1160,128]{1,0:T(8,128)}) %all-reduce.2.cloned.1.call-update) | async-done | bytes 593936 | tf_op jit(solution)/shard_map/psum | solution.py:98
  196.8 1.1 broadcast_multiply_fusion
  197.9 0.9 slice.164
  198.8 0.5 slice_bitcast_fusion.4
  (70 shorter events, 1.5 us)
Async XLA Ops:
  7.2 41.6 %copy-start = (bf16[1,1,32,32,128]{4,3,2,1,0:T(8,128)(2,1)S(1)}, bf16[1,1,32,32,128]{4,3,2,1,0:T(8,128)(2,1)}, u32[]{:S(2)}) copy-start(bf16[1,1,32,32,128]{4,3,2,1,0:T(8,128)(2,1)} %param.7) | copy-start | bytes 786436
  7.2 189.7 %all-reduce.2.cloned.1.call-start = ((), (), s32[]{:S(2)}) async-start(), calls=%async_computation | async-start | bytes 1187840 | tf_op jit(solution)/shard_map/psum | solution.py:98
  49.0 2.2 %copy-start.7 = (s32[128]{0:T(128)S(1)}, s32[128]{0:T(128)}, u32[]{:S(2)}) copy-start(s32[128]{0:T(128)} %param.13) | copy-start | bytes 1540
  49.0 2.2 %copy-start.8 = (s32[128,1]{0,1:T(1,128)S(1)}, s32[128,1]{0,1:T(1,128)}, u32[]{:S(2)}) copy-start(s32[128,1]{0,1:T(1,128)} %param.12) | copy-start | bytes 1540
  51.2 13.8 %copy-start.9 = (f32[128]{0:T(128)S(1)}, f32[128]{0:T(128)}, u32[]{:S(2)}) copy-start(f32[128]{0:T(128)} %param.9) | copy-start | bytes 1540
  51.2 13.5 %copy-start.2 = (bf16[32,32,128]{2,1,0:T(8,128)(2,1)S(1)}, bf16[32,32,128]{2,1,0:T(8,128)(2,1)}, u32[]{:S(2)}) copy-start(bf16[32,32,128]{2,1,0:T(8,128)(2,1)} %get-tuple-element.14) | copy-start | bytes 786436
  51.2 13.6 %copy-start.1 = (bf16[32,32,128]{2,1,0:T(8,128)(2,1)S(1)}, bf16[32,32,128]{2,1,0:T(8,128)(2,1)}, u32[]{:S(2)}) copy-start(bf16[32,32,128]{2,1,0:T(8,128)(2,1)} %get-tuple-element.13) | copy-start | bytes 786436
  51.2 13.8 %copy-start.3 = (bf16[9,128,128]{2,1,0:T(8,128)(2,1)S(1)}, bf16[9,128,128]{2,1,0:T(8,128)(2,1)}, u32[]{:S(2)}) copy-start(bf16[9,128,128]{2,1,0:T(8,128)(2,1)} %param.8) | copy-start | bytes 884740
  65.0 1.5 copy-start.5
  67.4 1.7 copy-start.4
  86.3 1.4 copy-start.6
Sparse Core Ops, SparseCore 0:
  69.3 127.5 all-reduce.1

commit v2 on v1

--- a/solution.py
+++ b/solution.py
@@ -66,12 +66,16 @@
     active = me < seam.shape[0] * grid * grid
     sources = rim_sources(seam)
 
-    sent = jnp.concatenate([edge_strips(field).reshape(4 * s, c), station_grad[0]], axis=0)
+    places = jnp.stack([station_tile[:, 0], station_cell // s, station_cell % s])
+    places = jnp.pad(places.reshape(-1, c), ((0, 16 - 3 * stations // c), (0, 0)))
+    sent = jnp.concatenate(
+        [edge_strips(field).reshape(4 * s, c), station_grad[0], places.astype(jnp.bfloat16)], axis=0)
     got = lax.all_gather(sent, GROUP, axis=0)
-    key = station_tile[:, 0] * (s * s) + station_cell
-    keys = lax.all_gather(key, GROUP, axis=0, tiled=True)
     lines = got[:, : 4 * s].reshape(slots, 4, s, c)
-    values = got[:, 4 * s :].reshape(slots * stations, c)
+    values = got[:, 4 * s : 4 * s + stations].reshape(slots * stations, c)
+    places = got[:, 4 * s + stations :].astype(jnp.int32).reshape(slots, -1)
+    part = [places[:, i * stations : (i + 1) * stations] for i in range(3)]
+    keys = (part[0] * (s * s) + part[1] * s + part[2]).reshape(-1)
 
     cols = patches(pad(field, lines, sources))
     preact = jnp.dot(cols, weight.reshape(9 * c, c), preferred_element_type=jnp.float32) + bias
@@ -93,10 +97,17 @@
     grad_w = lax.dot_general(
         cols, grad_pre, (((0,), (0,)), ((), ())), preferred_element_type=jnp.float32)
     grad_b = jnp.sum(grad_pre.astype(jnp.float32), axis=0, keepdims=True)
-    terms = jnp.concatenate([grad_w, jnp.broadcast_to(grad_b, (8, c))], axis=0)
-    terms = jnp.where(active, terms, 0.0)
-    total = lax.psum(terms, ("face", "tile", "dp"))
-    total = total / math.sqrt(lax.axis_size("dp") * slots * stations)
+    everyone = ("face", "tile", "dp")
+    devices = lax.axis_size(everyone)
+    rows = -(-(9 * c + 1) // (8 * devices)) * 8
+    terms = jnp.concatenate([grad_w, grad_b], axis=0)
+    terms = jnp.where(active, terms, 0.0).astype(jnp.bfloat16)
+    terms = jnp.pad(terms, ((0, rows * devices - terms.shape[0]), (0, 0)))
+    shares = lax.all_to_all(terms.reshape(devices, rows, c), everyone, 0, 0)
+    share = jnp.sum(shares.astype(jnp.float32), axis=0)
+    share = share / math.sqrt(lax.axis_size("dp") * slots * stations)
+    total = lax.all_gather(share.astype(jnp.bfloat16), everyone, axis=0, tiled=True)
+    total = total.astype(jnp.float32)
     return (output[None, None], grad_in[None, None],
             total[: 9 * c].reshape(9, c, c), total[9 * c])
 

time: 207 us -> 157 us (0.76)
  waiting for transfers between devices: 103 us -> 0.01 us
  blocking collectives: 45.8 us -> 107 us
  between operations: 32.2 us -> 18.8 us
  starting transfers between devices: 0.04 us -> 4.9 us
    psum x1 -> x0, waiting for transfers between devices: 103 us -> none  [body(): total = lax.psum(terms, ('face', 'tile', 'dp'))]
    all_gather x1, blocking collectives: 11.2 us -> 70.4 us  [body(): lax.all_gather(share.astype(jnp.bfloat16), everyone, axis=0, tiled=True)]
    all_to_all x0 -> x1, starting transfers between devices: none -> 4.9 us  [body(): shares = lax.all_to_all(terms.reshape(devices, rows, c), everyone, 0, 0)]
    unnamed x40 -> x37, local copies, waits for them, and re-layouts: 6.61 us -> 6.73 us
  transfers between devices with their start and end apart: 1 -> 1, of which waited for: 1 -> 0; matrix products, arithmetic and copies ran while one was open for 4% -> 5% of each run, Pallas kernels for 0% -> 0%
where the time goes in v2:
time: 157 us; the launch traced here: 156 us
  blocking collectives  107 us (68%)
  between operations  18.8 us (12%)
  local copies, waits for them, and re-layouts  16.1 us (10%)
  matrix products  6.39 us (4%)
  starting transfers between devices  4.9 us (3%)
  other arithmetic  3.26 us (2%)
    all_gather x1, blocking collectives, body(): lax.all_gather(share.astype(jnp.bfloat16), everyone, axis=0, tiled=True)  70.4 us
    all_gather x1, blocking collectives, body(): got = lax.all_gather(sent, GROUP, axis=0)  19.1 us
    all_gather x1, blocking collectives, body(): edges = lax.all_gather(edge_strips(grad_field), GROUP, axis=0)  17.2 us
    unnamed x37, local copies, waits for them, and re-layouts  6.73 us
    all_to_all x1, starting transfers between devices, body(): shares = lax.all_to_all(terms.reshape(devices, rows, c), everyone, 0, 0)  4.9 us
    dot_general x1, matrix products, body(): jnp.dot(patches(pad(grad_field, edges, sources)), flipped, preferred_elem...  3.15 us
  transfers between devices with their start and end apart: 1, of which 0 were waited for; matrix products, arithmetic and copies ran while one was open for 5% of the time, Pallas kernels for 0%

profile of v2, /device:TPU:0, one launch (start us, length us, event | category | flops | bytes accessed | tf_op | source)
XLA Modules:
  0.0 156.2 jit_solution(5856470784468787809)
XLA Ops:
  0.7 1.6 %constant_dynamic-slice_fusion.7 = (s32[1,1,1]{0,1,2:T(1,128)}, s32[1,1,1]{0,1,2:T(1,128)}, s32[1,1,1]{0,1,2:T(1,128)}, s32[1,1,1]{0,1,2:T(1,128)}, s32[1,1,1]{0...) fusion(s32[6,4,3]{0,1,2:T(4,128)} %param.10, ...), kind=kLoop, calls=%fused_computation.105 | loop fusion | bytes 100 | tf_op jit(solution)/shard_map/dynamic_slice | solution.py:26
  12.3 0.7 slice_bitcast_fusion.3
  13.0 0.9 fusion.34
  13.9 0.7 convert_bitcast_fusion.1
  14.6 0.7 convert_bitcast_fusion.2
  15.3 0.8 pad_maximum_fusion.6
  16.1 19.1 %all-gather = bf16[2176,128]{1,0:T(8,128)(2,1)S(1)} all-gather(bf16[272,128]{1,0:T(8,128)(2,1)S(1)} %pad_maximum_fusion.6), channel_id=2, replica_groups=mesh['face'=4,'tile'=2,'dp'=4] {'face','tile'}, dimensions={0}, use_global_device_ids=true | all-gather | bytes 626688 | tf_op jit(solution)/shard_map/all_gather | solution.py:73
  35.2 0.7 fusion.28
  43.8 0.2 pad_maximum_fusion.4
  44.1 0.2 pad_maximum_fusion
  44.3 1.0 fusion.32
  45.3 0.9 fusion.31
  46.3 1.1 constant_dynamic-update-slice_fusion.7
  47.3 1.0 constant_dynamic-update-slice_fusion.6
  48.8 1.5 select_convert_fusion
  50.4 0.9 convert_reduce_fusion.1
  51.3 0.8 fusion.35
  52.2 0.8 pad.10
  52.9 4.9 %all-to-all-start = ((bf16[32,40,128]{2,1,0:T(8,128)(2,1)}), bf16[32,40,128]{2,1,0:T(8,128)(2,1)S(1)}, u32[]{:S(2)}, u32[]{:S(2)}) async-start(bf16[32,40,128]{2,1,0:T(8,128)(2,1)} %bitcast.69), calls=%async_computation | async-start | bytes 655360 | tf_op jit(solution)/shard_map/all_to_all | solution.py:106
  57.9 0.2 copy.57
  58.2 17.2 %all-gather.1 = bf16[32,32,128]{2,1,0:T(8,128)(2,1)S(1)} all-gather(bf16[4,32,128]{2,1,0:T(8,128)(2,1)S(1)} %pad_maximum_fusion.8), channel_id=3, replica_groups=mesh['face'=4,'tile'=2,'dp'=4] {'face','tile'}, dimensions={0}, use_global_device_ids=true | all-gather | bytes 294912 | tf_op jit(solution)/shard_map/all_gather | solution.py:91
  75.6 0.2 pad_maximum_fusion.2
  75.8 0.2 pad_maximum_fusion.1
  76.6 1.4 copy-done.6
  78.2 0.7 constant_dynamic-update-slice_fusion.12
  78.9 0.8 constant_dynamic-update-slice_fusion.11
  79.7 0.7 constant_dynamic-update-slice_fusion.10
  80.4 0.8 constant_dynamic-update-slice_fusion.9
  81.2 3.1 %fusion.13 = bf16[1024,128]{1,0:T(8,128)(2,1)} fusion(bf16[1024,1152]{1,0:T(8,128)(2,1)} %constant_dynamic-update-slice_fusion.9, bf16[1152,128]{1,0:T(8,128)(2,1)S(1)} %bitcast.147, pred[]{:T(512)S(6)} %lt.32), kind=kOutput, calls=%fused_computation.9 | convolution fusion | flops 302252032 | bytes 2916353 | tf_op jit(solution)/shard_map/dot_general | solution.py:93
  84.4 70.4 %all_gather.19 = bf16[1280,128]{1,0:T(8,128)(2,1)S(1)} all-gather(bf16[40,128]{1,0:T(8,128)(2,1)S(1)} %multiply_convert_fusion), channel_id=1, replica_groups=mesh['face'=4,'tile'=2,'dp'=4] {'face','tile','dp'}, dimensions={0}, use_global_device_ids=true | all-gather | bytes 337920 | tf_op jit(solution)/shard_map/all_gather | solution.py:109
  154.8 0.9 slice.184
  155.7 0.5 slice_bitcast_fusion.4
  (72 shorter events, 1.8 us)
Async XLA Ops:
  0.6 43.2 %copy-start = (bf16[1,1,32,32,128]{4,3,2,1,0:T(8,128)(2,1)S(1)}, bf16[1,1,32,32,128]{4,3,2,1,0:T(8,128)(2,1)}, u32[]{:S(2)}) copy-start(bf16[1,1,32,32,128]{4,3,2,1,0:T(8,128)(2,1)} %param.7) | copy-start | bytes 786436
  46.2 2.6 %copy-start.7 = (f32[128]{0:T(128)S(1)}, f32[128]{0:T(128)}, u32[]{:S(2)}) copy-start(f32[128]{0:T(128)} %param.9) | copy-start | bytes 1540
  46.2 2.4 %copy-start.2 = (bf16[32,32,128]{2,1,0:T(8,128)(2,1)S(1)}, bf16[32,32,128]{2,1,0:T(8,128)(2,1)}, u32[]{:S(2)}) copy-start(bf16[32,32,128]{2,1,0:T(8,128)(2,1)} %get-tuple-element.14) | copy-start | bytes 786436
  46.2 2.4 %copy-start.1 = (bf16[32,32,128]{2,1,0:T(8,128)(2,1)S(1)}, bf16[32,32,128]{2,1,0:T(8,128)(2,1)}, u32[]{:S(2)}) copy-start(bf16[32,32,128]{2,1,0:T(8,128)(2,1)} %get-tuple-element.13) | copy-start | bytes 786436
  46.2 2.6 %copy-start.3 = (bf16[9,128,128]{2,1,0:T(8,128)(2,1)S(1)}, bf16[9,128,128]{2,1,0:T(8,128)(2,1)}, u32[]{:S(2)}) copy-start(bf16[9,128,128]{2,1,0:T(8,128)(2,1)} %param.8) | copy-start | bytes 884740
  48.8 1.5 copy-start.5
  51.3 6.6 %copy-start.4 = (bf16[9,128,128]{2,1,0:T(8,128)(2,1)S(1)}, bf16[9,128,128]{2,1,0:T(8,128)(2,1)}, u32[]{:S(2)}) copy-start(bf16[9,128,128]{2,1,0:T(8,128)(2,1)} %param.8) | copy-start | bytes 884740
  52.9 31.4 %all-to-all-start = ((bf16[32,40,128]{2,1,0:T(8,128)(2,1)}), bf16[32,40,128]{2,1,0:T(8,128)(2,1)S(1)}, u32[]{:S(2)}, u32[]{:S(2)}) async-start(bf16[32,40,128]{2,1,0:T(8,128)(2,1)} %bitcast.69), calls=%async_computation | async-start | bytes 655360 | tf_op jit(solution)/shard_map/all_to_all | solution.py:106
  76.5 1.4 copy-start.6
